TPU v7x, 32 devices: a whole 2x2x4 slice. The times are simulated.
32 devices in a mesh: span: 4 (over z), xs: 8 (over y, x, core).
Axes of the slice: x: 2, y: 2, z: 4, core: 2. Of those that a mesh axis runs over, the one named last changes fastest.
Arguments:
- source: float32 [64, 32, 2048], P(None, 'span', 'xs'), may hold values from -0.75 to 0.75
- coefficient: float32 [64, 32, 2048], P(None, 'span', 'xs'), may hold values from 2.5 to 5
- volume_matrix: float32 [64, 64], replicated, may hold values from -0.75 to 0.75
- span_lower: float32 [64, 64], replicated, may hold values from -0.375 to 0.375
- span_upper: float32 [64, 64], replicated, may hold values from -0.375 to 0.375
- cross_lower: float32 [64, 64], replicated, may hold values from -0.375 to 0.375
- cross_upper: float32 [64, 64], replicated, may hold values from -0.375 to 0.375
- interface: int32 [4, 8, 128], P('span', 'xs'), may hold values from 0 to 131071
- compliance: float32 [4, 1024, 1024], P('span', 'xs'), may hold values from -0.75 to 0.75
- start_displacement: float32 [4, 8, 128], P('span', 'xs'), may hold values from -8 to 8
Outputs:
- fluid_state: float32 [64, 32, 2048], P(None, 'span', 'xs')
- shell_displacement: float32 [4, 8, 128], P('span', 'xs')
All inputs are finite; a program needn't handle non-finite values.
Results may differ from a plain program's by a relative error of at most 0.0001.
Values sent between devices are 32-bit elements; how exact they have to be, the bound alone decides.
A program may use at most 64 MiB of HBM per device.

v0:
```python
import functools

import jax
import jax.numpy as jnp
from jax import lax
from jax.experimental import pallas as pl
from jax.experimental.pallas import tpu as pltpu
from jax.sharding import PartitionSpec as P

SUBITERS = 2
SHIFT = 3.75
LANES = 128
MESH = pl.DeviceIdType.MESH
f32, bf16 = jnp.float32, jnp.bfloat16


def split(value):
    high = value.astype(bf16)
    return high, (value - high.astype(f32)).astype(bf16)


def mm(a, b):
    return jnp.dot(a, b, preferred_element_type=f32)


def iota(shape, dim):
    return lax.broadcasted_iota(jnp.int32, shape, dim)


def to_column(row):
    k = row.shape[1]
    wide = jnp.broadcast_to(row, (k, k))
    keep = iota((k, k), 0) == iota((k, k), 1)
    return jnp.sum(jnp.where(keep, wide, jnp.zeros_like(wide)), axis=1, keepdims=True)


def to_row(column):
    k = column.shape[0]
    wide = jnp.broadcast_to(column, (k, k))
    keep = iota((k, k), 0) == iota((k, k), 1)
    return jnp.sum(jnp.where(keep, wide, jnp.zeros_like(wide)), axis=0, keepdims=True)


def window(dims, src, coef, vol, slo, sup, clo, cup, face, comp, disp0, out, dout,
           big, side, cs, base, fields, high, low, pick, pick_t, where_x,
           col_out, col_in, part, part_in, total, total_in,
           halo_send, halo_recv, xs_send, xs_recv, sp_send, sp_recv):
    nsp, nxs, N, S, X, K = dims
    sp, xs = lax.axis_index("span"), lax.axis_index("xs")
    barrier = pltpu.get_barrier_semaphore()
    for o in range(1, nxs):
        pl.semaphore_signal(barrier, inc=1, device_id={"xs": lax.rem(xs + o, nxs)}, device_id_type=MESH)
    for o in range(1, nsp):
        pl.semaphore_signal(barrier, inc=1, device_id={"span": lax.rem(sp + o, nsp)}, device_id_type=MESH)

    zero = jnp.zeros((N, N), f32)
    rows = jnp.concatenate([
        jnp.concatenate([-slo[...], vol[...], -sup[...]], axis=1),
        jnp.concatenate([zero, clo[...], zero], axis=1),
        jnp.concatenate([zero, cup[...], zero], axis=1),
    ], axis=0)
    bh, bl = split(rows)
    big[: 3 * N, :] = bh
    big[3 * N :, :] = bl
    for i, m in enumerate((clo, cup)):
        mh, ml = split(m[...])
        side[i, 0] = mh
        side[i, 1] = ml

    index_row = face[...]
    index_col = to_column(index_row.astype(f32)).astype(jnp.int32)

    def row_of(index):
        shift_x, shift_s = X.bit_length() - 1, S.bit_length() - 1
        s = (index >> shift_x) & (S - 1)
        return s * N + (index >> (shift_x + shift_s))

    hot = (iota((S * N, K), 0) == row_of(index_row)).astype(f32).astype(bf16)
    pick[:, :K] = hot
    pick[:, K:] = hot
    pick_t[...] = (iota((K, S * N), 1) == row_of(index_col)).astype(f32).astype(bf16)
    where_x[...] = (iota((K, X), 1) == (index_col & (X - 1))).astype(f32)

    for s in range(S):
        base[s * N : (s + 1) * N, :] = src[:, s, :]
        cs[s * N : (s + 1) * N, :] = coef[:, s, :] - SHIFT

    lane = iota((N, LANES), 1)
    wide = iota((N, X), 1)
    sent = []

    def own(s):
        return slice((s + 1) * N, (s + 2) * N)

    def start_halo(e):
        f, h, l = fields.at[e], high.at[e % 2], low.at[e % 2]
        copies = []

        def send(i, from_ref, to_ref, axis, target):
            c = pltpu.make_async_remote_copy(
                src_ref=from_ref, dst_ref=to_ref, send_sem=halo_send.at[e, i], recv_sem=halo_recv.at[e, i],
                device_id={axis: target}, device_id_type=MESH)
            c.start()
            copies.append(c)
            sent.append(c)

        up, down = lax.rem(sp + 1, nsp), lax.rem(sp + nsp - 1, nsp)
        right, left = lax.rem(xs + 1, nxs), lax.rem(xs + nxs - 1, nxs)
        send(0, f.at[pl.ds(S * N, N)], f.at[pl.ds(0, N)], "span", up)
        send(1, f.at[pl.ds(N, N)], f.at[pl.ds((S + 1) * N, N)], "span", down)
        first = jnp.zeros((N, LANES), f32)
        last = jnp.zeros((N, LANES), f32)
        for s in range(S):
            a = f[own(s), :LANES]
            b = f[own(s), X - LANES :]
            first = jnp.where(lane == s, pltpu.roll(a, s, 1) if s else a, first)
            last = jnp.where(lane == s, pltpu.roll(b, s + 1, 1), last)
        col_out[e, 0] = first
        col_out[e, 1] = last
        send(2, col_out.at[e, 1], col_in.at[e, 0], "xs", right)
        send(3, col_out.at[e, 0], col_in.at[e, 1], "xs", left)
        for s in range(S):
            h[own(s), :], l[own(s), :] = split(f[own(s), :])
        return copies

    def apply(e, target, copies):
        f, h, l = fields.at[e], high.at[e % 2], low.at[e % 2]

        def element_row(s):
            near = slice(s * N, (s + 3) * N)
            xh, xl = h[near, :], l[near, :]
            p = mm(big[...], xh)
            r = p[: 3 * N] + p[3 * N :] + mm(big[: 3 * N, :], xl)
            res = cs[s * N : (s + 1) * N, :] * f[own(s), :] + r[:N]
            res = res - jnp.where(wide == 0, 0.0, pltpu.roll(r[N : 2 * N], 1, 1))
            res = res - jnp.where(wide == X - 1, 0.0, pltpu.roll(r[2 * N :], X - 1, 1))
            target[own(s), :] = res

        for s in range(1, S - 1):
            element_row(s)
        for c in copies:
            c.wait_recv()
        for row in (slice(0, N), slice((S + 1) * N, (S + 2) * N)):
            h[row, :], l[row, :] = split(f[row, :])
        element_row(0)
        element_row(S - 1)
        edges = []
        for i, there in enumerate((xs > 0, xs < nxs - 1)):
            got = jnp.where(there, col_in[e, i], 0.0)
            gh, gl = split(got)
            edges.append(mm(side[i, 0], gh) + mm(side[i, 1], gh) + mm(side[i, 0], gl))
        for s in range(S):
            first = pltpu.roll(edges[0], LANES - s, 1) if s else edges[0]
            target[own(s), :LANES] = target[own(s), :LANES] - jnp.where(lane == 0, first, 0.0)
            last = pltpu.roll(edges[1], LANES - 1 - s, 1)
            target[own(s), X - LANES :] = target[own(s), X - LANES :] - jnp.where(lane == LANES - 1, last, 0.0)

    def traces(e):
        h, l = high.at[e % 2], low.at[e % 2]
        body = slice(N, (S + 1) * N)
        t = mm(pick_t[...], h[body, :]) + mm(pick_t[...], l[body, :])
        return to_row(jnp.sum(t * where_x[...], axis=1, keepdims=True))

    def fold(v):
        v = jnp.sum(v, axis=0, keepdims=True)
        return functools.reduce(lambda a, b: a + b, [v[:, i : i + LANES] for i in range(0, X, LANES)])

    def products(pairs):
        res = []
        for a, b in pairs:
            acc = None
            for s in range(S):
                t = a[own(s), :] * b[own(s), :]
                acc = t if acc is None else acc + t
            res.append(fold(acc))
        return res

    d = to_column(disp0[...])
    for sub in range(SUBITERS):
        er, ew = 2 * sub, 2 * sub + 1
        r, w, u = fields.at[er], fields.at[ew], fields.at[2 * SUBITERS]
        dh, dl = split(d * where_x[...])
        push = jnp.concatenate([dh, dl], axis=0)
        for s in range(S):
            r[own(s), :] = base[s * N : (s + 1) * N, :] + mm(pick[s * N : (s + 1) * N, :], push)
        if sub == 0:
            pl.semaphore_wait(barrier, nxs + nsp - 2)
        copies = start_halo(er)
        apply(er, w, copies)
        copies = start_halo(ew)
        rt, wt = traces(er), traces(ew)
        rr, rw, ww = products([(r, r), (r, w), (w, w)])
        apply(ew, u, copies)
        ru, wu, uu = products([(r, u), (w, u), (u, u)])
        mine = jnp.concatenate([rt, wt, rr, rw, ru, ww, wu, uu], axis=0)
        part[sub] = mine
        copies = []
        for o in range(1, nxs):
            c = pltpu.make_async_remote_copy(
                src_ref=part.at[sub], dst_ref=part_in.at[sub, xs],
                send_sem=xs_send.at[sub, o], recv_sem=xs_recv.at[sub, o],
                device_id={"xs": lax.rem(xs + o, nxs)}, device_id_type=MESH)
            c.start()
            copies.append(c)
            sent.append(c)
        part_in[sub, xs] = mine
        for c in copies:
            c.wait_recv()
        acc = part_in[sub, 0]
        for i in range(1, nxs):
            acc = acc + part_in[sub, i]
        total[sub] = acc
        copies = []
        for o in range(1, nsp):
            c = pltpu.make_async_remote_copy(
                src_ref=total.at[sub], dst_ref=total_in.at[sub, sp],
                send_sem=sp_send.at[sub, o], recv_sem=sp_recv.at[sub, o],
                device_id={"span": lax.rem(sp + o, nsp)}, device_id_type=MESH)
            c.start()
            copies.append(c)
            sent.append(c)
        total_in[sub, sp] = acc
        y = []
        for j in range(2):
            a = jnp.zeros((comp.shape[0], K), f32)
            for i in range(nxs):
                a = a + comp[:, i * K : (i + 1) * K] * part_in[sub, i, j : j + 1, :]
            y.append(jnp.sum(a, axis=1, keepdims=True))
        for c in copies:
            c.wait_recv()
        acc = total_in[sub, 0]
        for i in range(1, nsp):
            acc = acc + total_in[sub, i]
        g = jnp.sum(acc, axis=1, keepdims=True)
        rr, rw, ru, ww, wu, uu = [g[i : i + 1, :] for i in range(2, 8)]
        c0 = SHIFT
        g11 = ww + 2.0 * c0 * rw + c0 * c0 * rr
        g12 = wu + c0 * (ww + ru) + c0 * c0 * rw
        g22 = uu + 2.0 * c0 * wu + c0 * c0 * ww
        b1 = rw + c0 * rr
        b2 = ru + c0 * rw
        det = g11 * g22 - g12 * g12
        ca = (b1 * g22 - b2 * g12) / det
        cb = (b2 * g11 - b1 * g12) / det
        d = 0.5 * (ca * y[0] + cb * y[1]) + 0.5 * d
    for s in range(S):
        out[s * N : (s + 1) * N, :] = ca * r[own(s), :] + cb * w[own(s), :]
    dout[...] = to_row(d)
    for c in sent:
        c.wait_send()


def body(nsp, nxs, source, coefficient, volume, slo, sup, clo, cup, interface, compliance, start):
    N, S, X = source.shape
    K = interface.shape[2]
    M = compliance.shape[1]
    E = 2 * SUBITERS
    vm = pl.BlockSpec(memory_space=pltpu.VMEM)
    tall = (S + 2) * N
    dma = pltpu.SemaphoreType.DMA
    out, disp = pl.pallas_call(
        functools.partial(window, (nsp, nxs, N, S, X, K)),
        out_shape=(jax.ShapeDtypeStruct((S * N, X), f32), jax.ShapeDtypeStruct((1, K), f32)),
        in_specs=[vm] * 10,
        out_specs=(vm, vm),
        scratch_shapes=[
            pltpu.VMEM((6 * N, 3 * N), bf16),
            pltpu.VMEM((2, 2, N, N), bf16),
            pltpu.VMEM((S * N, X), f32),
            pltpu.VMEM((S * N, X), f32),
            pltpu.VMEM((E + 1, tall, X), f32),
            pltpu.VMEM((2, tall, X), bf16),
            pltpu.VMEM((2, tall, X), bf16),
            pltpu.VMEM((S * N, 2 * K), bf16),
            pltpu.VMEM((K, S * N), bf16),
            pltpu.VMEM((K, X), f32),
            pltpu.VMEM((E, 2, N, LANES), f32),
            pltpu.VMEM((E, 2, N, LANES), f32),
            pltpu.VMEM((SUBITERS, 8, LANES), f32),
            pltpu.VMEM((SUBITERS, nxs, 8, LANES), f32),
            pltpu.VMEM((SUBITERS, 8, LANES), f32),
            pltpu.VMEM((SUBITERS, nsp, 8, LANES), f32),
            dma((E, 4)), dma((E, 4)),
            dma((SUBITERS, nxs)), dma((SUBITERS, nxs)),
            dma((SUBITERS, nsp)), dma((SUBITERS, nsp)),
        ],
        compiler_params=pltpu.CompilerParams(
            collective_id=0, has_side_effects=True, vmem_limit_bytes=40 * 1024 * 1024),
        cost_estimate=pl.CostEstimate(flops=2 ** 30, bytes_accessed=2 ** 21, transcendentals=0),
        name="coupling_window",
    )(source, coefficient, volume, slo, sup, clo, cup,
      interface.reshape(1, K), compliance.reshape(M, compliance.shape[2]), start.reshape(1, K))
    return out.reshape(S, N, X).transpose(1, 0, 2), disp.reshape(1, 1, K)


def solution(mesh):
    field, shell = P(None, "span", "xs"), P("span", "xs", None)
    return jax.shard_map(
        functools.partial(body, mesh.shape["span"], mesh.shape["xs"]),
        mesh=mesh,
        in_specs=(field, field, P(), P(), P(), P(), P(), shell, shell, shell),
        out_specs=(field, shell),
        check_vma=False,
    )
```

profile of v0, /device:TPU:0, one launch (start us, length us, event | category | flops | bytes accessed | tf_op | source)
XLA Modules:
  0.0 50.7 jit_solution(18252033021601924416)
XLA Ops:
  0.6 0.0 copy-start.8
  0.6 0.0 copy-start.9
  0.7 0.6 %copy-done.8 = s32[1,1,128]{2,1,0:T(1,128)S(1)} copy-done((s32[1,1,128]{2,1,0:T(1,128)S(1)}, s32[1,1,128]{2,1,0:T(1,128)}, u32[]{:S(2)}) %copy-start.8) | copy-done | bytes 536
  1.3 0.0 copy-done.9
  1.3 0.0 copy-start
  1.3 1.0 %copy-done = f32[64,8,256]{2,1,0:T(8,128)S(1)} copy-done((f32[64,8,256]{2,1,0:T(8,128)S(1)}, f32[64,8,256]{2,1,0:T(8,128)}, u32[]{:S(2)}) %copy-start) | copy-done | bytes 524312
  2.3 0.0 copy-start.1
  2.4 1.0 %copy-done.1 = f32[64,8,256]{2,1,0:T(8,128)S(1)} copy-done((f32[64,8,256]{2,1,0:T(8,128)S(1)}, f32[64,8,256]{2,1,0:T(8,128)}, u32[]{:S(2)}) %copy-start.1) | copy-done | bytes 524312
  3.4 0.0 copy-start.2
  3.4 1.0 %copy-done.2 = f32[1,128,1024]{2,1,0:T(8,128)S(1)} copy-done((f32[1,128,1024]{2,1,0:T(8,128)S(1)}, f32[1,128,1024]{2,1,0:T(8,128)}, u32[]{:S(2)}) %copy-start.2) | copy-done | bytes 524312
  4.4 0.0 copy-start.3
  4.4 0.8 %copy-done.3 = f32[64,64]{1,0:T(8,128)S(1)} copy-done((f32[64,64]{1,0:T(8,128)S(1)}, f32[64,64]{1,0:T(8,128)}, u32[]{:S(2)}) %copy-start.3) | copy-done | bytes 16408
  5.2 0.0 copy-start.4
  5.2 0.8 %copy-done.4 = f32[64,64]{1,0:T(8,128)S(1)} copy-done((f32[64,64]{1,0:T(8,128)S(1)}, f32[64,64]{1,0:T(8,128)}, u32[]{:S(2)}) %copy-start.4) | copy-done | bytes 16408
  5.9 0.0 copy-start.5
  6.0 0.8 %copy-done.5 = f32[64,64]{1,0:T(8,128)S(1)} copy-done((f32[64,64]{1,0:T(8,128)S(1)}, f32[64,64]{1,0:T(8,128)}, u32[]{:S(2)}) %copy-start.5) | copy-done | bytes 16408
  6.7 0.0 copy-start.6
  6.7 0.8 %copy-done.6 = f32[64,64]{1,0:T(8,128)S(1)} copy-done((f32[64,64]{1,0:T(8,128)S(1)}, f32[64,64]{1,0:T(8,128)}, u32[]{:S(2)}) %copy-start.6) | copy-done | bytes 16408
  7.5 0.0 copy-start.7
  7.5 0.8 %copy-done.7 = f32[64,64]{1,0:T(8,128)S(1)} copy-done((f32[64,64]{1,0:T(8,128)S(1)}, f32[64,64]{1,0:T(8,128)}, u32[]{:S(2)}) %copy-start.7) | copy-done | bytes 16408
  8.2 40.8 %coupling_window.1 = (f32[512,256]{1,0:T(8,128)S(1)}, f32[1,128]{1,0:T(1,128)S(1)}) custom-call(f32[64,8,256]{2,1,0:T(8,128)S(1)} %copy-done, f32[64,8,256]{2,1,0:T(8,128)S(1)} %copy-done.1, f32[64,64]{1,0:T(8,128)S(1)} %copy-done.3, f32[64,64]{1,0:T(8,128)S(1)} %copy-done.4, f32[64,64]{1,0:T(8,128)S(1)} %copy-done.5, f32[64,64]{1,0:T(8,128)S(1)} %copy-done.6, ...), custom_call_target="tpu_custom_call" | custom-call | flops 1073741824 | bytes 2097152 | tf_op jit(solution)/shard_map/coupling_window/pallas_call | solution.py:261
  49.1 1.1 %copy.14 = f32[8,64,256]{2,0,1:T(8,128)} copy(f32[8,64,256]{2,1,0:T(8,128)S(1)} %bitcast.8) | data formatting | bytes 1048576 | tf_op jit(solution)/shard_map/reshape | solution.py:293
  50.2 0.5 %copy.16 = f32[1,1,128]{2,1,0:T(1,128)} copy(f32[1,1,128]{2,1,0:T(1,128)S(1)} %bitcast.12) | data formatting | bytes 1024
Async XLA Ops:
  0.6 0.7 %copy-start.8 = (s32[1,1,128]{2,1,0:T(1,128)S(1)}, s32[1,1,128]{2,1,0:T(1,128)}, u32[]{:S(2)}) copy-start(s32[1,1,128]{2,1,0:T(1,128)} %param.17) | copy-start | bytes 1540
  0.6 0.7 %copy-start.9 = (f32[1,1,128]{2,1,0:T(1,128)S(1)}, f32[1,1,128]{2,1,0:T(1,128)}, u32[]{:S(2)}) copy-start(f32[1,1,128]{2,1,0:T(1,128)} %param.19) | copy-start | bytes 1540
  1.3 1.0 %copy-start = (f32[64,8,256]{2,1,0:T(8,128)S(1)}, f32[64,8,256]{2,1,0:T(8,128)}, u32[]{:S(2)}) copy-start(f32[64,8,256]{2,1,0:T(8,128)} %src.1) | copy-start | bytes 1572868
  2.3 1.0 %copy-start.1 = (f32[64,8,256]{2,1,0:T(8,128)S(1)}, f32[64,8,256]{2,1,0:T(8,128)}, u32[]{:S(2)}) copy-start(f32[64,8,256]{2,1,0:T(8,128)} %coef.1) | copy-start | bytes 1572868
  3.4 1.0 %copy-start.2 = (f32[1,128,1024]{2,1,0:T(8,128)S(1)}, f32[1,128,1024]{2,1,0:T(8,128)}, u32[]{:S(2)}) copy-start(f32[1,128,1024]{2,1,0:T(8,128)} %param.18) | copy-start | bytes 1572868
  4.4 0.8 %copy-start.3 = (f32[64,64]{1,0:T(8,128)S(1)}, f32[64,64]{1,0:T(8,128)}, u32[]{:S(2)}) copy-start(f32[64,64]{1,0:T(8,128)} %vol.1) | copy-start | bytes 49156
  5.2 0.8 %copy-start.4 = (f32[64,64]{1,0:T(8,128)S(1)}, f32[64,64]{1,0:T(8,128)}, u32[]{:S(2)}) copy-start(f32[64,64]{1,0:T(8,128)} %slo.1) | copy-start | bytes 49156
  5.9 0.8 %copy-start.5 = (f32[64,64]{1,0:T(8,128)S(1)}, f32[64,64]{1,0:T(8,128)}, u32[]{:S(2)}) copy-start(f32[64,64]{1,0:T(8,128)} %sup.1) | copy-start | bytes 49156
  6.7 0.8 %copy-start.6 = (f32[64,64]{1,0:T(8,128)S(1)}, f32[64,64]{1,0:T(8,128)}, u32[]{:S(2)}) copy-start(f32[64,64]{1,0:T(8,128)} %clo.1) | copy-start | bytes 49156
  7.5 0.8 %copy-start.7 = (f32[64,64]{1,0:T(8,128)S(1)}, f32[64,64]{1,0:T(8,128)}, u32[]{:S(2)}) copy-start(f32[64,64]{1,0:T(8,128)} %cup.1) | copy-start | bytes 49156
where the time goes:
time: 51.3 us; the launch traced here: 50.7 us
  Pallas kernels  40.8 us (80%)
  local copies, waits for them, and re-layouts  9.18 us (18%)
  between operations  0.67 us (1%)
    pallas_call x1, Pallas kernels, body(): pl.pallas_call(functools.partial(window, (nsp, nxs, N, S, X, K)), out_sha...  40.8 us
    unnamed x21, local copies, waits for them, and re-layouts  8.08 us
    reshape x1, local copies, waits for them, and re-layouts, body(): return (out.reshape(S, N, X).transpose(1, 0, 2), disp.reshape(1, 1, K))  1.1 us

commit v1 on v0

--- a/solution.py
+++ b/solution.py
@@ -41,10 +41,21 @@
     return jnp.sum(jnp.where(keep, wide, jnp.zeros_like(wide)), axis=0, keepdims=True)
 
 
-def window(dims, src, coef, vol, slo, sup, clo, cup, face, comp, disp0, out, dout,
-           big, side, cs, base, fields, high, low, pick, pick_t, where_x,
+def window(dims, *refs):
+    given, refs = refs[:10], refs[10:]
+    out, dout, refs = refs[0], refs[1], refs[2:]
+    held, refs = refs[:10], refs[10:]
+    run_window(dims, given, held, out, dout, *refs)
+
+
+def run_window(dims, given, held, out, dout, big, side, cs, base, fields, high, low, pick, pick_t, where_x,
            col_out, col_in, part, part_in, total, total_in,
-           halo_send, halo_recv, xs_send, xs_recv, sp_send, sp_recv):
+           halo_send, halo_recv, xs_send, xs_recv, sp_send, sp_recv,
+           note_out, note_in, in_sem, out_sem):
+    src, coef, vol, slo, sup, clo, cup, face, comp, disp0 = held
+    fetch = [pltpu.make_async_copy(a, b, in_sem.at[i]) for i, (a, b) in enumerate(zip(given, held))]
+    for i in (0, 7, 9, 2, 3, 4, 5, 6, 1, 8):
+        fetch[i].start()
     nsp, nxs, N, S, X, K = dims
     sp, xs = lax.axis_index("span"), lax.axis_index("xs")
     barrier = pltpu.get_barrier_semaphore()
@@ -52,6 +63,9 @@
         pl.semaphore_signal(barrier, inc=1, device_id={"xs": lax.rem(xs + o, nxs)}, device_id_type=MESH)
     for o in range(1, nsp):
         pl.semaphore_signal(barrier, inc=1, device_id={"span": lax.rem(sp + o, nsp)}, device_id_type=MESH)
+
+    for i in (2, 3, 4, 5, 6, 7, 9):
+        fetch[i].wait()
 
     zero = jnp.zeros((N, N), f32)
     rows = jnp.concatenate([
@@ -70,8 +84,9 @@
     index_row = face[...]
     index_col = to_column(index_row.astype(f32)).astype(jnp.int32)
 
+    shift_x, shift_s = X.bit_length() - 1, S.bit_length() - 1
+
     def row_of(index):
-        shift_x, shift_s = X.bit_length() - 1, S.bit_length() - 1
         s = (index >> shift_x) & (S - 1)
         return s * N + (index >> (shift_x + shift_s))
 
@@ -81,6 +96,8 @@
     pick_t[...] = (iota((K, S * N), 1) == row_of(index_col)).astype(f32).astype(bf16)
     where_x[...] = (iota((K, X), 1) == (index_col & (X - 1))).astype(f32)
 
+    fetch[0].wait()
+    fetch[1].wait()
     for s in range(S):
         base[s * N : (s + 1) * N, :] = src[:, s, :]
         cs[s * N : (s + 1) * N, :] = coef[:, s, :] - SHIFT
@@ -92,38 +109,98 @@
     def own(s):
         return slice((s + 1) * N, (s + 2) * N)
 
-    def start_halo(e):
-        f, h, l = fields.at[e], high.at[e % 2], low.at[e % 2]
-        copies = []
-
-        def send(i, from_ref, to_ref, axis, target):
-            c = pltpu.make_async_remote_copy(
-                src_ref=from_ref, dst_ref=to_ref, send_sem=halo_send.at[e, i], recv_sem=halo_recv.at[e, i],
-                device_id={axis: target}, device_id_type=MESH)
-            c.start()
-            copies.append(c)
-            sent.append(c)
-
-        up, down = lax.rem(sp + 1, nsp), lax.rem(sp + nsp - 1, nsp)
-        right, left = lax.rem(xs + 1, nxs), lax.rem(xs + nxs - 1, nxs)
-        send(0, f.at[pl.ds(S * N, N)], f.at[pl.ds(0, N)], "span", up)
-        send(1, f.at[pl.ds(N, N)], f.at[pl.ds((S + 1) * N, N)], "span", down)
+    def own_ds(s):
+        return pl.ds((s + 1) * N, N)
+
+    up, down = lax.rem(sp + 1, nsp), lax.rem(sp + nsp - 1, nsp)
+    right, left = lax.rem(xs + 1, nxs), lax.rem(xs + nxs - 1, nxs)
+    towards = (("span", up), ("span", down), ("xs", right), ("xs", left))
+    order = [0, S - 1] + list(range(1, S - 1))
+
+    def send(e, i, from_ref, to_ref):
+        axis, target = towards[i]
+        c = pltpu.make_async_remote_copy(
+            src_ref=from_ref, dst_ref=to_ref, send_sem=halo_send.at[e, i], recv_sem=halo_recv.at[e, i],
+            device_id={axis: target}, device_id_type=MESH)
+        c.start()
+        sent.append(c)
+        return c
+
+    def split_own(e, s):
+        high[e % 2, own(s), :], low[e % 2, own(s), :] = split(fields[e, own(s), :])
+
+    def split_halo(e):
+        for row in (slice(0, N), slice((S + 1) * N, (S + 2) * N)):
+            high[e % 2, row, :], low[e % 2, row, :] = split(fields[e, row, :])
+
+    def start_halo(e, fill):
+        f = fields.at[e]
+        fill(0)
+        fill(S - 1)
+        if e == 0:
+            pl.semaphore_wait(barrier, nxs + nsp - 2)
+        copies = [
+            send(e, 0, f.at[pl.ds(S * N, N)], f.at[pl.ds(0, N)]),
+            send(e, 1, f.at[pl.ds(N, N)], f.at[pl.ds((S + 1) * N, N)]),
+        ]
         first = jnp.zeros((N, LANES), f32)
         last = jnp.zeros((N, LANES), f32)
-        for s in range(S):
+        for s in order:
+            if 0 < s < S - 1:
+                fill(s)
             a = f[own(s), :LANES]
             b = f[own(s), X - LANES :]
             first = jnp.where(lane == s, pltpu.roll(a, s, 1) if s else a, first)
             last = jnp.where(lane == s, pltpu.roll(b, s + 1, 1), last)
         col_out[e, 0] = first
         col_out[e, 1] = last
-        send(2, col_out.at[e, 1], col_in.at[e, 0], "xs", right)
-        send(3, col_out.at[e, 0], col_in.at[e, 1], "xs", left)
+        copies.append(send(e, 2, col_out.at[e, 1], col_in.at[e, 0]))
+        copies.append(send(e, 3, col_out.at[e, 0], col_in.at[e, 1]))
         for s in range(S):
-            h[own(s), :], l[own(s), :] = split(f[own(s), :])
-        return copies
-
-    def apply(e, target, copies):
+            split_own(e, s)
+
+        def finish():
+            for c in copies:
+                c.wait_recv()
+            split_halo(e)
+
+        return finish
+
+    def start_change(e, change, fill):
+        note_out[e // 2] = jnp.concatenate(
+            [index_row.astype(f32), to_row(change), jnp.zeros((6, K), f32)], axis=0)
+        copies = [send(e, i, note_out.at[e // 2], note_in.at[e // 2, i]) for i in range(4)]
+        for s in range(S):
+            fill(s)
+            split_own(e, s)
+
+        def finish():
+            for c in copies:
+                c.wait_recv()
+            for i in range(4):
+                there = note_in[e // 2, i]
+                at_row = there[0:1].astype(jnp.int32)
+                at = to_column(there[0:1]).astype(jnp.int32)
+                by = to_column(there[1:2])
+                if i < 2:
+                    s, halo = ((S - 1, 0), (0, S + 1))[i]
+                    hot = (iota((N, K), 0) + s * N == row_of(at_row)).astype(f32).astype(bf16)
+                    vh, vl = split(jnp.where(iota((K, X), 1) == (at & (X - 1)), by, 0.0))
+                    halo = slice(halo * N, (halo + 1) * N)
+                    fields[e, halo, :] = fields[e - 2, halo, :] + (mm(hot, vh) + mm(hot, vl))
+                else:
+                    edge = (X - 1, 0)[i - 2]
+                    node = at_row >> (shift_x + shift_s)
+                    hot = (iota((N, K), 0) == node).astype(f32).astype(bf16)
+                    by = jnp.where((at & (X - 1)) == edge, by, 0.0)
+                    s_of = (at >> shift_x) & (S - 1)
+                    vh, vl = split(jnp.where(iota((K, LANES), 1) == s_of, by, 0.0))
+                    col_in[e, i - 2] = col_in[e - 2, i - 2] + (mm(hot, vh) + mm(hot, vl))
+            split_halo(e)
+
+        return finish
+
+    def apply(e, target, finish):
         f, h, l = fields.at[e], high.at[e % 2], low.at[e % 2]
 
         def element_row(s):
@@ -138,10 +215,7 @@
 
         for s in range(1, S - 1):
             element_row(s)
-        for c in copies:
-            c.wait_recv()
-        for row in (slice(0, N), slice((S + 1) * N, (S + 2) * N)):
-            h[row, :], l[row, :] = split(f[row, :])
+        finish()
         element_row(0)
         element_row(S - 1)
         edges = []
@@ -149,11 +223,14 @@
             got = jnp.where(there, col_in[e, i], 0.0)
             gh, gl = split(got)
             edges.append(mm(side[i, 0], gh) + mm(side[i, 1], gh) + mm(side[i, 0], gl))
-        for s in range(S):
+
+        def fill(s):
             first = pltpu.roll(edges[0], LANES - s, 1) if s else edges[0]
             target[own(s), :LANES] = target[own(s), :LANES] - jnp.where(lane == 0, first, 0.0)
             last = pltpu.roll(edges[1], LANES - 1 - s, 1)
             target[own(s), X - LANES :] = target[own(s), X - LANES :] - jnp.where(lane == LANES - 1, last, 0.0)
+
+        return fill
 
     def traces(e):
         h, l = high.at[e % 2], low.at[e % 2]
@@ -181,16 +258,17 @@
         r, w, u = fields.at[er], fields.at[ew], fields.at[2 * SUBITERS]
         dh, dl = split(d * where_x[...])
         push = jnp.concatenate([dh, dl], axis=0)
-        for s in range(S):
+
+        def fill_rhs(s):
             r[own(s), :] = base[s * N : (s + 1) * N, :] + mm(pick[s * N : (s + 1) * N, :], push)
-        if sub == 0:
-            pl.semaphore_wait(barrier, nxs + nsp - 2)
-        copies = start_halo(er)
-        apply(er, w, copies)
-        copies = start_halo(ew)
+
+        finish = start_change(er, change, fill_rhs) if sub else start_halo(er, fill_rhs)
+        finish = start_halo(ew, apply(er, w, finish))
         rt, wt = traces(er), traces(ew)
         rr, rw, ww = products([(r, r), (r, w), (w, w)])
-        apply(ew, u, copies)
+        fill = apply(ew, u, finish)
+        for s in range(S):
+            fill(s)
         ru, wu, uu = products([(r, u), (w, u), (u, u)])
         mine = jnp.concatenate([rt, wt, rr, rw, ru, ww, wu, uu], axis=0)
         part[sub] = mine
@@ -220,6 +298,8 @@
             copies.append(c)
             sent.append(c)
         total_in[sub, sp] = acc
+        if sub == 0:
+            fetch[8].wait()
         y = []
         for j in range(2):
             a = jnp.zeros((comp.shape[0], K), f32)
@@ -242,12 +322,19 @@
         det = g11 * g22 - g12 * g12
         ca = (b1 * g22 - b2 * g12) / det
         cb = (b2 * g11 - b1 * g12) / det
+        change = 0.5 * (ca * y[0] + cb * y[1]) - 0.5 * d
         d = 0.5 * (ca * y[0] + cb * y[1]) + 0.5 * d
+    leaving = []
     for s in range(S):
-        out[s * N : (s + 1) * N, :] = ca * r[own(s), :] + cb * w[own(s), :]
+        u[own(s), :] = ca * r[own(s), :] + cb * w[own(s), :]
+        c = pltpu.make_async_copy(u.at[own_ds(s)], out.at[pl.ds(s * N, N)], out_sem.at[s])
+        c.start()
+        leaving.append(c)
     dout[...] = to_row(d)
     for c in sent:
         c.wait_send()
+    for c in leaving:
+        c.wait()
 
 
 def body(nsp, nxs, source, coefficient, volume, slo, sup, clo, cup, interface, compliance, start):
@@ -256,14 +343,17 @@
     M = compliance.shape[1]
     E = 2 * SUBITERS
     vm = pl.BlockSpec(memory_space=pltpu.VMEM)
+    hbm = pl.BlockSpec(memory_space=pltpu.HBM)
     tall = (S + 2) * N
     dma = pltpu.SemaphoreType.DMA
+    args = (source, coefficient, volume, slo, sup, clo, cup,
+            interface.reshape(1, K), compliance.reshape(M, compliance.shape[2]), start.reshape(1, K))
     out, disp = pl.pallas_call(
         functools.partial(window, (nsp, nxs, N, S, X, K)),
         out_shape=(jax.ShapeDtypeStruct((S * N, X), f32), jax.ShapeDtypeStruct((1, K), f32)),
-        in_specs=[vm] * 10,
-        out_specs=(vm, vm),
-        scratch_shapes=[
+        in_specs=[hbm] * 10,
+        out_specs=(hbm, vm),
+        scratch_shapes=[pltpu.VMEM(a.shape, a.dtype) for a in args] + [
             pltpu.VMEM((6 * N, 3 * N), bf16),
             pltpu.VMEM((2, 2, N, N), bf16),
             pltpu.VMEM((S * N, X), f32),
@@ -283,13 +373,15 @@
             dma((E, 4)), dma((E, 4)),
             dma((SUBITERS, nxs)), dma((SUBITERS, nxs)),
             dma((SUBITERS, nsp)), dma((SUBITERS, nsp)),
+            pltpu.VMEM((SUBITERS, 8, K), f32),
+            pltpu.VMEM((SUBITERS, 4, 8, K), f32),
+            dma((10,)), dma((S,)),
         ],
         compiler_params=pltpu.CompilerParams(
             collective_id=0, has_side_effects=True, vmem_limit_bytes=40 * 1024 * 1024),
         cost_estimate=pl.CostEstimate(flops=2 ** 30, bytes_accessed=2 ** 21, transcendentals=0),
         name="coupling_window",
-    )(source, coefficient, volume, slo, sup, clo, cup,
-      interface.reshape(1, K), compliance.reshape(M, compliance.shape[2]), start.reshape(1, K))
+    )(*args)
     return out.reshape(S, N, X).transpose(1, 0, 2), disp.reshape(1, 1, K)
 
 

time: 51.3 us -> 52.2 us (1.018)
  Pallas kernels: 40.8 us -> 41.7 us
    pallas_call x1, Pallas kernels: 40.8 us -> 41.7 us  [body(): pl.pallas_call(functools.partial(window, (nsp, nxs, N, S, X, K)), out_sha...]
where the time goes in v1:
time: 52.2 us; the launch traced here: 51.6 us
  Pallas kernels  41.7 us (80%)
  local copies, waits for them, and re-layouts  9.18 us (18%)
  between operations  0.67 us (1%)
    pallas_call x1, Pallas kernels, body(): pl.pallas_call(functools.partial(window, (nsp, nxs, N, S, X, K)), out_sha...  41.7 us
    unnamed x21, local copies, waits for them, and re-layouts  8.08 us
    reshape x1, local copies, waits for them, and re-layouts, body(): return (out.reshape(S, N, X).transpose(1, 0, 2), disp.reshape(1, 1, K))  1.1 us

profile of v1, /device:TPU:0, one launch (start us, length us, event | category | flops | bytes accessed | tf_op | source)
XLA Modules:
  0.0 51.6 jit_solution(14305175299373240480)
XLA Ops:
  0.6 0.0 copy-start.8
  0.6 0.0 copy-start.9
  0.7 0.6 %copy-done.8 = s32[1,1,128]{2,1,0:T(1,128)S(1)} copy-done((s32[1,1,128]{2,1,0:T(1,128)S(1)}, s32[1,1,128]{2,1,0:T(1,128)}, u32[]{:S(2)}) %copy-start.8) | copy-done | bytes 536
  1.3 0.0 copy-done.9
  1.3 0.0 copy-start
  1.3 1.0 %copy-done = f32[64,8,256]{2,1,0:T(8,128)S(1)} copy-done((f32[64,8,256]{2,1,0:T(8,128)S(1)}, f32[64,8,256]{2,1,0:T(8,128)}, u32[]{:S(2)}) %copy-start) | copy-done | bytes 524312
  2.3 0.0 copy-start.1
  2.4 1.0 %copy-done.1 = f32[64,8,256]{2,1,0:T(8,128)S(1)} copy-done((f32[64,8,256]{2,1,0:T(8,128)S(1)}, f32[64,8,256]{2,1,0:T(8,128)}, u32[]{:S(2)}) %copy-start.1) | copy-done | bytes 524312
  3.4 0.0 copy-start.2
  3.4 1.0 %copy-done.2 = f32[1,128,1024]{2,1,0:T(8,128)S(1)} copy-done((f32[1,128,1024]{2,1,0:T(8,128)S(1)}, f32[1,128,1024]{2,1,0:T(8,128)}, u32[]{:S(2)}) %copy-start.2) | copy-done | bytes 524312
  4.4 0.0 copy-start.3
  4.4 0.8 %copy-done.3 = f32[64,64]{1,0:T(8,128)S(1)} copy-done((f32[64,64]{1,0:T(8,128)S(1)}, f32[64,64]{1,0:T(8,128)}, u32[]{:S(2)}) %copy-start.3) | copy-done | bytes 16408
  5.2 0.0 copy-start.4
  5.2 0.8 %copy-done.4 = f32[64,64]{1,0:T(8,128)S(1)} copy-done((f32[64,64]{1,0:T(8,128)S(1)}, f32[64,64]{1,0:T(8,128)}, u32[]{:S(2)}) %copy-start.4) | copy-done | bytes 16408
  5.9 0.0 copy-start.5
  6.0 0.8 %copy-done.5 = f32[64,64]{1,0:T(8,128)S(1)} copy-done((f32[64,64]{1,0:T(8,128)S(1)}, f32[64,64]{1,0:T(8,128)}, u32[]{:S(2)}) %copy-start.5) | copy-done | bytes 16408
  6.7 0.0 copy-start.6
  6.7 0.8 %copy-done.6 = f32[64,64]{1,0:T(8,128)S(1)} copy-done((f32[64,64]{1,0:T(8,128)S(1)}, f32[64,64]{1,0:T(8,128)}, u32[]{:S(2)}) %copy-start.6) | copy-done | bytes 16408
  7.5 0.0 copy-start.7
  7.5 0.8 %copy-done.7 = f32[64,64]{1,0:T(8,128)S(1)} copy-done((f32[64,64]{1,0:T(8,128)S(1)}, f32[64,64]{1,0:T(8,128)}, u32[]{:S(2)}) %copy-start.7) | copy-done | bytes 16408
  8.2 41.7 %coupling_window.1 = (f32[512,256]{1,0:T(8,128)S(1)}, f32[1,128]{1,0:T(1,128)S(1)}) custom-call(f32[64,8,256]{2,1,0:T(8,128)S(1)} %copy-done, f32[64,8,256]{2,1,0:T(8,128)S(1)} %copy-done.1, f32[64,64]{1,0:T(8,128)S(1)} %copy-done.3, f32[64,64]{1,0:T(8,128)S(1)} %copy-done.4, f32[64,64]{1,0:T(8,128)S(1)} %copy-done.5, f32[64,64]{1,0:T(8,128)S(1)} %copy-done.6, ...), custom_call_target="tpu_custom_call" | custom-call | flops 1073741824 | bytes 2097152 | tf_op jit(solution)/shard_map/coupling_window/pallas_call | solution.py:351
  50.0 1.1 %copy.14 = f32[8,64,256]{2,0,1:T(8,128)} copy(f32[8,64,256]{2,1,0:T(8,128)S(1)} %bitcast.8) | data formatting | bytes 1048576 | tf_op jit(solution)/shard_map/reshape | solution.py:385
  51.1 0.5 copy.16
Async XLA Ops:
  0.6 0.7 %copy-start.8 = (s32[1,1,128]{2,1,0:T(1,128)S(1)}, s32[1,1,128]{2,1,0:T(1,128)}, u32[]{:S(2)}) copy-start(s32[1,1,128]{2,1,0:T(1,128)} %param.17) | copy-start | bytes 1540
  0.6 0.7 %copy-start.9 = (f32[1,1,128]{2,1,0:T(1,128)S(1)}, f32[1,1,128]{2,1,0:T(1,128)}, u32[]{:S(2)}) copy-start(f32[1,1,128]{2,1,0:T(1,128)} %param.19) | copy-start | bytes 1540
  1.3 1.0 %copy-start = (f32[64,8,256]{2,1,0:T(8,128)S(1)}, f32[64,8,256]{2,1,0:T(8,128)}, u32[]{:S(2)}) copy-start(f32[64,8,256]{2,1,0:T(8,128)} %refs_0_.1) | copy-start | bytes 1572868
  2.3 1.0 %copy-start.1 = (f32[64,8,256]{2,1,0:T(8,128)S(1)}, f32[64,8,256]{2,1,0:T(8,128)}, u32[]{:S(2)}) copy-start(f32[64,8,256]{2,1,0:T(8,128)} %refs_1_.1) | copy-start | bytes 1572868
  3.4 1.0 %copy-start.2 = (f32[1,128,1024]{2,1,0:T(8,128)S(1)}, f32[1,128,1024]{2,1,0:T(8,128)}, u32[]{:S(2)}) copy-start(f32[1,128,1024]{2,1,0:T(8,128)} %param.18) | copy-start | bytes 1572868
  4.4 0.8 %copy-start.3 = (f32[64,64]{1,0:T(8,128)S(1)}, f32[64,64]{1,0:T(8,128)}, u32[]{:S(2)}) copy-start(f32[64,64]{1,0:T(8,128)} %refs_2_.1) | copy-start | bytes 49156
  5.2 0.8 %copy-start.4 = (f32[64,64]{1,0:T(8,128)S(1)}, f32[64,64]{1,0:T(8,128)}, u32[]{:S(2)}) copy-start(f32[64,64]{1,0:T(8,128)} %refs_3_.1) | copy-start | bytes 49156
  5.9 0.8 %copy-start.5 = (f32[64,64]{1,0:T(8,128)S(1)}, f32[64,64]{1,0:T(8,128)}, u32[]{:S(2)}) copy-start(f32[64,64]{1,0:T(8,128)} %refs_4_.1) | copy-start | bytes 49156
  6.7 0.8 %copy-start.6 = (f32[64,64]{1,0:T(8,128)S(1)}, f32[64,64]{1,0:T(8,128)}, u32[]{:S(2)}) copy-start(f32[64,64]{1,0:T(8,128)} %refs_5_.1) | copy-start | bytes 49156
  7.5 0.8 %copy-start.7 = (f32[64,64]{1,0:T(8,128)S(1)}, f32[64,64]{1,0:T(8,128)}, u32[]{:S(2)}) copy-start(f32[64,64]{1,0:T(8,128)} %refs_6_.1) | copy-start | bytes 49156

commit v2 on v1

--- a/solution.py
+++ b/solution.py
@@ -378,7 +378,7 @@
             dma((10,)), dma((S,)),
         ],
         compiler_params=pltpu.CompilerParams(
-            collective_id=0, has_side_effects=True, vmem_limit_bytes=40 * 1024 * 1024),
+            collective_id=0, has_side_effects=True, vmem_limit_bytes=64 * 1024 * 1024),
         cost_estimate=pl.CostEstimate(flops=2 ** 30, bytes_accessed=2 ** 21, transcendentals=0),
         name="coupling_window",
     )(*args)

time: 52.2 us -> 46.5 us (0.89)
  local copies, waits for them, and re-layouts: 9.18 us -> 3.32 us
  Pallas kernels: 41.7 us -> 42.3 us
    unnamed x21 -> x3, local copies, waits for them, and re-layouts: 8.08 us -> 1.18 us
    reshape x1, local copies, waits for them, and re-layouts: 1.1 us -> 2.14 us  [body(): return (out.reshape(S, N, X).transpose(1, 0, 2), disp.reshape(1, 1, K))]
    pallas_call x1, Pallas kernels: 41.7 us -> 42.3 us  [body(): pl.pallas_call(functools.partial(window, (nsp, nxs, N, S, X, K)), out_sha...]
where the time goes in v2:
time: 46.5 us; the launch traced here: 46.3 us
  Pallas kernels  42.3 us (91%)
  local copies, waits for them, and re-layouts  3.32 us (7%)
  between operations  0.64 us (1%)
    pallas_call x1, Pallas kernels, body(): pl.pallas_call(functools.partial(window, (nsp, nxs, N, S, X, K)), out_sha...  42.3 us
    reshape x1, local copies, waits for them, and re-layouts, body(): return (out.reshape(S, N, X).transpose(1, 0, 2), disp.reshape(1, 1, K))  2.14 us
    unnamed x3, local copies, waits for them, and re-layouts  1.18 us

profile of v2, /device:TPU:0, one launch (start us, length us, event | category | flops | bytes accessed | tf_op | source)
XLA Modules:
  0.0 46.3 jit_solution(16686049015264600461)
XLA Ops:
  0.6 42.3 %coupling_window.1 = (f32[512,256]{1,0:T(8,128)}, f32[1,128]{1,0:T(1,128)}) custom-call(f32[64,8,256]{2,1,0:T(8,128)} %refs_0_.1, f32[64,8,256]{2,1,0:T(8,128)} %refs_1_.1, f32[64,64]{1,0:T(8,128)} %refs_2_.1, f32[64,64]{1,0:T(8,128)} %refs_3_.1, f32[64,64]{1,0:T(8,128)} %refs_4_.1, f32[64,64]{1,0:T(8,128)} %refs_5_.1, f32[64,64]{1,0:T(8,128)} %refs_6_.1, ...), custom_call_target="tpu_custom_call" | custom-call | flops 1073741824 | bytes 2097152 | tf_op jit(solution)/shard_map/coupling_window/pallas_call | solution.py:351
  43.0 2.1 %copy.14 = f32[8,64,256]{2,0,1:T(8,128)} copy(f32[8,64,256]{2,1,0:T(8,128)} %bitcast.9) | data formatting | bytes 1048576 | tf_op jit(solution)/shard_map/reshape | solution.py:385
  45.1 0.0 copy-start
  45.1 0.7 %copy-done = f32[1,128]{1,0:T(1,128)S(1)} copy-done((f32[1,128]{1,0:T(1,128)S(1)}, f32[1,128]{1,0:T(1,128)}, u32[]{:S(2)}) %copy-start) | copy-done | bytes 536
  45.8 0.5 %copy.16 = f32[1,1,128]{2,1,0:T(1,128)} copy(f32[1,1,128]{2,1,0:T(1,128)S(1)} %bitcast.13) | data formatting | bytes 1024
Async XLA Ops:
  45.1 0.7 %copy-start = (f32[1,128]{1,0:T(1,128)S(1)}, f32[1,128]{1,0:T(1,128)}, u32[]{:S(2)}) copy-start(f32[1,128]{1,0:T(1,128)} %get-tuple-element.5) | copy-start | bytes 1540

commit v3 on v2

--- a/solution.py
+++ b/solution.py
@@ -64,22 +64,8 @@
     for o in range(1, nsp):
         pl.semaphore_signal(barrier, inc=1, device_id={"span": lax.rem(sp + o, nsp)}, device_id_type=MESH)
 
-    for i in (2, 3, 4, 5, 6, 7, 9):
-        fetch[i].wait()
-
-    zero = jnp.zeros((N, N), f32)
-    rows = jnp.concatenate([
-        jnp.concatenate([-slo[...], vol[...], -sup[...]], axis=1),
-        jnp.concatenate([zero, clo[...], zero], axis=1),
-        jnp.concatenate([zero, cup[...], zero], axis=1),
-    ], axis=0)
-    bh, bl = split(rows)
-    big[: 3 * N, :] = bh
-    big[3 * N :, :] = bl
-    for i, m in enumerate((clo, cup)):
-        mh, ml = split(m[...])
-        side[i, 0] = mh
-        side[i, 1] = ml
+    fetch[7].wait()
+    fetch[9].wait()
 
     index_row = face[...]
     index_col = to_column(index_row.astype(f32)).astype(jnp.int32)
@@ -90,17 +76,29 @@
         s = (index >> shift_x) & (S - 1)
         return s * N + (index >> (shift_x + shift_s))
 
-    hot = (iota((S * N, K), 0) == row_of(index_row)).astype(f32).astype(bf16)
-    pick[:, :K] = hot
-    pick[:, K:] = hot
-    pick_t[...] = (iota((K, S * N), 1) == row_of(index_col)).astype(f32).astype(bf16)
+    place = row_of(index_row)
     where_x[...] = (iota((K, X), 1) == (index_col & (X - 1))).astype(f32)
 
-    fetch[0].wait()
-    fetch[1].wait()
-    for s in range(S):
-        base[s * N : (s + 1) * N, :] = src[:, s, :]
-        cs[s * N : (s + 1) * N, :] = coef[:, s, :] - SHIFT
+    def prepare():
+        for i in range(2, 7):
+            fetch[i].wait()
+        zero = jnp.zeros((N, N), f32)
+        rows = jnp.concatenate([
+            jnp.concatenate([-slo[...], vol[...], -sup[...]], axis=1),
+            jnp.concatenate([zero, clo[...], zero], axis=1),
+            jnp.concatenate([zero, cup[...], zero], axis=1),
+        ], axis=0)
+        bh, bl = split(rows)
+        big[: 3 * N, :] = bh
+        big[3 * N :, :] = bl
+        for i, m in enumerate((clo, cup)):
+            mh, ml = split(m[...])
+            side[i, 0] = mh
+            side[i, 1] = ml
+        pick_t[...] = (iota((K, S * N), 1) == row_of(index_col)).astype(f32).astype(bf16)
+        fetch[1].wait()
+        for s in range(S):
+            cs[s * N : (s + 1) * N, :] = coef[:, s, :] - SHIFT
 
     lane = iota((N, LANES), 1)
     wide = iota((N, X), 1)
@@ -108,9 +106,6 @@
 
     def own(s):
         return slice((s + 1) * N, (s + 2) * N)
-
-    def own_ds(s):
-        return pl.ds((s + 1) * N, N)
 
     up, down = lax.rem(sp + 1, nsp), lax.rem(sp + nsp - 1, nsp)
     right, left = lax.rem(xs + 1, nxs), lax.rem(xs + nxs - 1, nxs)
@@ -253,6 +248,7 @@
         return res
 
     d = to_column(disp0[...])
+    fetch[0].wait()
     for sub in range(SUBITERS):
         er, ew = 2 * sub, 2 * sub + 1
         r, w, u = fields.at[er], fields.at[ew], fields.at[2 * SUBITERS]
@@ -260,9 +256,17 @@
         push = jnp.concatenate([dh, dl], axis=0)
 
         def fill_rhs(s):
-            r[own(s), :] = base[s * N : (s + 1) * N, :] + mm(pick[s * N : (s + 1) * N, :], push)
+            mine = slice(s * N, (s + 1) * N)
+            if sub == 0:
+                hot = (iota((N, K), 0) + s * N == place).astype(f32).astype(bf16)
+                pick[mine, :K] = hot
+                pick[mine, K:] = hot
+                base[mine, :] = src[:, s, :]
+            r[own(s), :] = base[mine, :] + mm(pick[mine, :], push)
 
         finish = start_change(er, change, fill_rhs) if sub else start_halo(er, fill_rhs)
+        if sub == 0:
+            prepare()
         finish = start_halo(ew, apply(er, w, finish))
         rt, wt = traces(er), traces(ew)
         rr, rw, ww = products([(r, r), (r, w), (w, w)])
@@ -324,17 +328,14 @@
         cb = (b2 * g11 - b1 * g12) / det
         change = 0.5 * (ca * y[0] + cb * y[1]) - 0.5 * d
         d = 0.5 * (ca * y[0] + cb * y[1]) + 0.5 * d
-    leaving = []
     for s in range(S):
-        u[own(s), :] = ca * r[own(s), :] + cb * w[own(s), :]
-        c = pltpu.make_async_copy(u.at[own_ds(s)], out.at[pl.ds(s * N, N)], out_sem.at[s])
-        c.start()
-        leaving.append(c)
-    dout[...] = to_row(d)
+        src[:, s, :] = ca * r[own(s), :] + cb * w[own(s), :]
+    leaving = pltpu.make_async_copy(src, out, out_sem)
+    leaving.start()
+    dout[0] = to_row(d)
     for c in sent:
         c.wait_send()
-    for c in leaving:
-        c.wait()
+    leaving.wait()
 
 
 def body(nsp, nxs, source, coefficient, volume, slo, sup, clo, cup, interface, compliance, start):
@@ -350,7 +351,7 @@
             interface.reshape(1, K), compliance.reshape(M, compliance.shape[2]), start.reshape(1, K))
     out, disp = pl.pallas_call(
         functools.partial(window, (nsp, nxs, N, S, X, K)),
-        out_shape=(jax.ShapeDtypeStruct((S * N, X), f32), jax.ShapeDtypeStruct((1, K), f32)),
+        out_shape=(jax.ShapeDtypeStruct((N, S, X), f32), jax.ShapeDtypeStruct((1, 1, K), f32)),
         in_specs=[hbm] * 10,
         out_specs=(hbm, vm),
         scratch_shapes=[pltpu.VMEM(a.shape, a.dtype) for a in args] + [
@@ -375,14 +376,14 @@
             dma((SUBITERS, nsp)), dma((SUBITERS, nsp)),
             pltpu.VMEM((SUBITERS, 8, K), f32),
             pltpu.VMEM((SUBITERS, 4, 8, K), f32),
-            dma((10,)), dma((S,)),
+            dma((10,)), dma,
         ],
         compiler_params=pltpu.CompilerParams(
             collective_id=0, has_side_effects=True, vmem_limit_bytes=64 * 1024 * 1024),
         cost_estimate=pl.CostEstimate(flops=2 ** 30, bytes_accessed=2 ** 21, transcendentals=0),
         name="coupling_window",
     )(*args)
-    return out.reshape(S, N, X).transpose(1, 0, 2), disp.reshape(1, 1, K)
+    return out, disp
 
 
 def solution(mesh):

time: 46.5 us -> 45.2 us (0.972)
  local copies, waits for them, and re-layouts: 3.32 us -> 2.38 us
    reshape x1 -> x0, local copies, waits for them, and re-layouts: 2.14 us -> none  [body(): return (out.reshape(S, N, X).transpose(1, 0, 2), disp.reshape(1, 1, K))]
    unnamed x3 -> x4, local copies, waits for them, and re-layouts: 1.18 us -> 2.38 us
where the time goes in v3:
time: 45.2 us; the launch traced here: 45 us
  Pallas kernels  42 us (93%)
  local copies, waits for them, and re-layouts  2.38 us (5%)
  between operations  0.65 us (1%)
    pallas_call x1, Pallas kernels, body(): pl.pallas_call(functools.partial(window, (nsp, nxs, N, S, X, K)), out_sha...  42 us
    unnamed x4, local copies, waits for them, and re-layouts  2.38 us

profile of v3, /device:TPU:0, one launch (start us, length us, event | category | flops | bytes accessed | tf_op | source)
XLA Modules:
  0.0 45.0 jit_solution(2465347684678837101)
XLA Ops:
  0.6 42.0 %coupling_window.1 = (f32[64,8,256]{2,1,0:T(8,128)}, f32[1,1,128]{2,1,0:T(1,128)}) custom-call(f32[64,8,256]{2,1,0:T(8,128)} %refs_0_.1, f32[64,8,256]{2,1,0:T(8,128)} %refs_1_.1, f32[64,64]{1,0:T(8,128)} %refs_2_.1, f32[64,64]{1,0:T(8,128)} %refs_3_.1, f32[64,64]{1,0:T(8,128)} %refs_4_.1, f32[64,64]{1,0:T(8,128)} %refs_5_.1, f32[64,64]{1,0:T(8,128)} %refs_6_.1, ...), custom_call_target="tpu_custom_call" | custom-call | flops 1073741824 | bytes 2097152 | tf_op jit(solution)/shard_map/coupling_window/pallas_call | solution.py:352
  42.6 0.0 copy-start
  42.7 1.9 %copy.14 = f32[64,8,256]{2,1,0:T(8,128)} copy(f32[64,8,256]{2,1,0:T(8,128)} %get-tuple-element.4) | data formatting | bytes 1048576
  44.5 0.0 copy-done
  44.5 0.5 %copy.15 = f32[1,1,128]{2,1,0:T(1,128)} copy(f32[1,1,128]{2,1,0:T(1,128)S(1)} %copy-done) | data formatting | bytes 1024
Async XLA Ops:
  42.6 1.9 %copy-start = (f32[1,1,128]{2,1,0:T(1,128)S(1)}, f32[1,1,128]{2,1,0:T(1,128)}, u32[]{:S(2)}) copy-start(f32[1,1,128]{2,1,0:T(1,128)} %get-tuple-element.5) | copy-start | bytes 1540

commit v4 on v3

--- a/solution.py
+++ b/solution.py
@@ -170,9 +170,8 @@
             split_own(e, s)
 
         def finish():
-            for c in copies:
-                c.wait_recv()
-            for i in range(4):
+            for i in (2, 3, 0, 1):
+                copies[i].wait_recv()
                 there = note_in[e // 2, i]
                 at_row = there[0:1].astype(jnp.int32)
                 at = to_column(there[0:1]).astype(jnp.int32)

time: 45.2 us -> 45.6 us (level)
  no operation moved by 1% of the time
where the time goes in v4:
time: 45.6 us; the launch traced here: 45.4 us
  Pallas kernels  42.4 us (93%)
  local copies, waits for them, and re-layouts  2.38 us (5%)
  between operations  0.65 us (1%)
    pallas_call x1, Pallas kernels, body(): pl.pallas_call(functools.partial(window, (nsp, nxs, N, S, X, K)), out_sha...  42.4 us
    unnamed x4, local copies, waits for them, and re-layouts  2.38 us

profile of v4, /device:TPU:0, one launch (start us, length us, event | category | flops | bytes accessed | tf_op | source)
XLA Modules:
  0.0 45.4 jit_solution(6192034768393077097)
XLA Ops:
  0.6 42.4 %coupling_window.1 = (f32[64,8,256]{2,1,0:T(8,128)}, f32[1,1,128]{2,1,0:T(1,128)}) custom-call(f32[64,8,256]{2,1,0:T(8,128)} %refs_0_.1, f32[64,8,256]{2,1,0:T(8,128)} %refs_1_.1, f32[64,64]{1,0:T(8,128)} %refs_2_.1, f32[64,64]{1,0:T(8,128)} %refs_3_.1, f32[64,64]{1,0:T(8,128)} %refs_4_.1, f32[64,64]{1,0:T(8,128)} %refs_5_.1, f32[64,64]{1,0:T(8,128)} %refs_6_.1, ...), custom_call_target="tpu_custom_call" | custom-call | flops 1073741824 | bytes 2097152 | tf_op jit(solution)/shard_map/coupling_window/pallas_call | solution.py:351
  43.0 0.0 copy-start
  43.0 1.9 %copy.14 = f32[64,8,256]{2,1,0:T(8,128)} copy(f32[64,8,256]{2,1,0:T(8,128)} %get-tuple-element.4) | data formatting | bytes 1048576
  44.9 0.0 copy-done
  44.9 0.5 %copy.15 = f32[1,1,128]{2,1,0:T(1,128)} copy(f32[1,1,128]{2,1,0:T(1,128)S(1)} %copy-done) | data formatting | bytes 1024
Async XLA Ops:
  43.0 1.9 %copy-start = (f32[1,1,128]{2,1,0:T(1,128)S(1)}, f32[1,1,128]{2,1,0:T(1,128)}, u32[]{:S(2)}) copy-start(f32[1,1,128]{2,1,0:T(1,128)} %get-tuple-element.5) | copy-start | bytes 1540
